TPU v7x, 32 devices: a whole 2x2x4 slice. The times are simulated.
32 devices in a mesh: dp: 2 (over x), row: 4 (over z), col: 4 (over y, core).
Axes of the slice: x: 2, y: 2, z: 4, core: 2. Of those that a mesh axis runs over, the one named last changes fastest.
Arguments:
- query_out: bfloat16 [384, 4096], P(('dp', 'row'), 'col'), may hold values from -6 to 6
- query_in: bfloat16 [384, 4096], P(('dp', 'col')), may hold values from -6 to 6
- out_basis: bfloat16 [4096, 4096], P('col', ('dp', 'row')), may hold values from -0.09375 to 0.09375
- in_basis: bfloat16 [4096, 4096], P(('dp', 'row'), 'col'), may hold values from -0.09375 to 0.09375
- eigvals: float32 [4096, 4096], P(('dp', 'row'), 'col'), may hold values from 16 to 1024
- train_out: bfloat16 [384, 4096], P(('dp', 'row'), 'col'), may hold values from -0.09375 to 0.09375
- train_in: bfloat16 [384, 4096], P(('dp', 'col')), may hold values from -0.09375 to 0.09375
Outputs:
- precond: float32 [4096, 4096], P(('dp', 'row'), 'col')
- scores: float32 [384], P('dp')
All inputs are finite; a program needn't handle non-finite values.
Results may differ from a plain program's by a relative error of at most 0.028.
Values may be sent and summed in bfloat16 or wider, within the bound.
A program may use at most 64 MiB of HBM per device.

v0:
```python
import jax
import jax.numpy as jnp
from jax import lax
from jax.sharding import PartitionSpec as P

damping = 1.0


def rotate_out(tok_rows, basis_panel):
    gathered = lax.all_gather(tok_rows, "row", axis=0, tiled=True)
    partial_sum = jnp.dot(gathered, basis_panel, preferred_element_type=jnp.float32)
    return lax.psum(partial_sum.astype(jnp.bfloat16), "col")


def rotate_in(tok_rows, basis_panel):
    groups = lax.axis_size("dp")
    row_count = lax.axis_size("row")
    sub_width = tok_rows.shape[1] // (groups * row_count)
    split_rows = tok_rows.reshape(tok_rows.shape[0], groups, row_count, sub_width)
    picked = lax.dynamic_index_in_dim(split_rows, lax.axis_index("row"), 2, keepdims=False)
    picked = picked.reshape(tok_rows.shape[0], groups * sub_width)
    gathered = lax.all_gather(picked, "col", axis=0, tiled=True)
    partial_sum = jnp.dot(gathered, basis_panel, preferred_element_type=jnp.float32)
    return lax.psum(partial_sum.astype(jnp.bfloat16), "row")


def per_device(query_out, query_in, out_basis, in_basis, eigvals, train_out, train_in):
    panel_out = lax.all_gather(out_basis, "dp", axis=1, tiled=True)
    panel_in = lax.all_gather(in_basis, "dp", axis=0, tiled=True)
    query_rot = rotate_out(query_out, panel_out)
    query_inr = rotate_in(query_in, panel_in)
    partial_grad = lax.dot_general(
        query_rot, query_inr, (((0,), (0,)), ((), ())), preferred_element_type=jnp.float32
    )
    owned = lax.psum_scatter(
        partial_grad.astype(jnp.bfloat16), "dp", scatter_dimension=0, tiled=True
    ).astype(jnp.float32)
    precond = owned / (eigvals + damping)
    shared = precond.astype(jnp.bfloat16)
    train_rot = rotate_out(train_out, panel_out)
    train_inr = rotate_in(train_in, panel_in)
    mixed = jnp.dot(
        train_rot,
        lax.all_gather(shared, "dp", axis=0, tiled=True),
        preferred_element_type=jnp.float32,
    )
    partial_scores = jnp.sum(mixed * train_inr.astype(jnp.float32), axis=1)
    scores = lax.psum(partial_scores, ("row", "col"))
    return (precond, scores)


def solution(mesh):
    in_specs = (
        P(("dp", "row"), "col"),
        P(("dp", "col"), None),
        P("col", ("dp", "row")),
        P(("dp", "row"), "col"),
        P(("dp", "row"), "col"),
        P(("dp", "row"), "col"),
        P(("dp", "col"), None),
    )
    out_specs = (P(("dp", "row"), "col"), P("dp"))
    return jax.shard_map(
        per_device, mesh=mesh, in_specs=in_specs, out_specs=out_specs, check_vma=False
    )
```

profile of v0, /device:TPU:0, one launch (start us, length us, event | category | flops | bytes accessed | tf_op | source)
XLA Modules:
  0.0 278.3 jit_solution(8362768689654486158)
XLA Ops:
  7.2 0.0 copy-start.3
  7.2 0.0 copy-start.4
  7.2 0.0 copy-start.5
  7.2 0.0 all-gather.4.cloned.1.call-start
  7.2 0.7 all-gather.4.cloned.1.call-update
  7.9 0.0 copy-start.6
  7.9 0.0 all-gather.6.cloned.1.call-start
  8.0 0.7 all-gather.6.cloned.1.call-update
  8.7 0.0 all-reduce.5.cloned.1.call-start
  8.7 0.0 copy-done.3
  8.7 0.3 reshape.18
  9.0 0.0 copy-done.4
  9.0 0.3 reshape.20
  9.3 1.4 dynamic-slice_reduce_fusion
  10.7 0.0 copy-done.5
  10.7 16.2 %all_gather.21 = bf16[192,1024]{1,0:T(8,128)(2,1)S(1)} all-gather(bf16[48,1024]{1,0:T(8,128)(2,1)S(1)} %copy-done.5), channel_id=1, replica_groups=mesh['dp'=2,'row'=4,'col'=4] {'row'}, dimensions={0}, use_global_device_ids=true | all-gather | bytes 491520 | tf_op jit(solution)/shard_map/all_gather | solution.py:10
  27.0 0.0 copy-done.6
  27.0 15.4 %all_gather.25 = bf16[192,1024]{1,0:T(8,128)(2,1)S(1)} all-gather(bf16[48,1024]{1,0:T(8,128)(2,1)S(1)} %copy-done.6), channel_id=1, replica_groups=mesh['dp'=2,'row'=4,'col'=4] {'row'}, dimensions={0}, use_global_device_ids=true | all-gather | bytes 491520 | tf_op jit(solution)/shard_map/all_gather | solution.py:10
  42.4 6.5 %all_gather.23 = bf16[192,1024]{1,0:T(8,128)(2,1)S(1)} all-gather(bf16[48,1024]{1,0:T(8,128)(2,1)S(1)} %bitcast.19), channel_id=1, replica_groups=mesh['dp'=2,'row'=4,'col'=4] {'col'}, dimensions={0}, use_global_device_ids=true | all-gather | bytes 491520 | tf_op jit(solution)/shard_map/all_gather | solution.py:22
  48.9 6.6 %all_gather.27 = bf16[192,1024]{1,0:T(8,128)(2,1)S(1)} all-gather(bf16[48,1024]{1,0:T(8,128)(2,1)S(1)} %bitcast.16), channel_id=1, replica_groups=mesh['dp'=2,'row'=4,'col'=4] {'col'}, dimensions={0}, use_global_device_ids=true | all-gather | bytes 491520 | tf_op jit(solution)/shard_map/all_gather | solution.py:22
  55.5 0.0 all-gather.4.cloned.1.call-done
  55.5 0.0 copy-start.1
  55.5 3.3 %convolution_convert_fusion.4 = bf16[192,1024]{1,0:T(8,128)(2,1)} fusion(bf16[192,1024]{1,0:T(8,128)(2,1)S(1)} %all_gather.21, bf16[1024,1024]{1,0:T(8,128)(2,1)} %all-gather.4.cloned.1.call-done), kind=kOutput, calls=%fused_computation.6 | convolution fusion | flops 402849792 | bytes 2883584 | tf_op jit(solution)/shard_map/dot_general | solution.py:11
  58.7 0.0 copy-done.1
  58.7 1.4 convolution_convert_fusion.2
  60.1 0.0 all-reduce.5.cloned.1.call-update
  60.1 0.0 all-reduce.7.cloned.1.call-start
  60.2 20.0 %all-gather.6.cloned.1.call-done = bf16[1024,1024]{1,0:T(8,128)(2,1)} async-done(((bf16[512,1024]{1,0:T(8,128)(2,1)}), bf16[1024,1024]{1,0:T(8,128)(2,1)}) %all-gather.6.cloned.1.call-update) | async-done | bytes 2097168 | tf_op jit(solution)/shard_map/all_gather | solution.py:29
  80.1 0.0 copy-start
  80.1 3.1 %convolution_convert_fusion.3 = bf16[192,1024]{1,0:T(8,128)(2,1)} fusion(bf16[192,1024]{1,0:T(8,128)(2,1)S(1)} %all_gather.23, bf16[1024,1024]{1,0:T(8,128)(2,1)} %all-gather.6.cloned.1.call-done), kind=kOutput, calls=%fused_computation.5 | convolution fusion | flops 402849792 | bytes 2883584 | tf_op jit(solution)/shard_map/dot_general | solution.py:23
  83.2 0.0 copy-done
  83.2 1.3 convolution_convert_fusion.1
  84.5 0.0 all-reduce.7.cloned.1.call-update
  84.5 0.0 reduce-scatter.2.cloned.1.call-start
  84.6 33.2 %all-reduce.5.cloned.1.call-done = (bf16[192,1024]{1,0:T(8,128)(2,1)}, bf16[192,1024]{1,0:T(8,128)(2,1)}) async-done(((bf16[192,1024]{1,0:T(8,128)(2,1)}, bf16[192,1024]{1,0:T(8,128)(2,1)}), (bf16[192,1024]{1,0:T(8,128)(2,1)}, bf16[192,1024]{1,0:T(8,128)(2,1)})) %all-reduce.5.cloned.1.call-update) | async-done | bytes 786448 | tf_op jit(solution)/shard_map/psum | solution.py:12
  117.8 46.5 %all-reduce.7.cloned.1.call-done = (bf16[192,1024]{1,0:T(8,128)(2,1)}, bf16[192,1024]{1,0:T(8,128)(2,1)}) async-done(((bf16[192,1024]{1,0:T(8,128)(2,1)}, bf16[192,1024]{1,0:T(8,128)(2,1)}), (bf16[192,1024]{1,0:T(8,128)(2,1)}, bf16[192,1024]{1,0:T(8,128)(2,1)})) %all-reduce.7.cloned.1.call-update) | async-done | bytes 786448 | tf_op jit(solution)/shard_map/psum | solution.py:24
  164.3 0.0 copy-start.2
  164.3 3.3 %convolution_convert_fusion = bf16[1024,1024]{1,0:T(8,128)(2,1)} fusion(bf16[192,1024]{1,0:T(8,128)(2,1)} %get-tuple-element.2, bf16[192,1024]{1,0:T(8,128)(2,1)} %get-tuple-element.4), kind=kOutput, calls=%fused_computation.1 | convolution fusion | flops 403701760 | bytes 2883584 | tf_op jit(solution)/shard_map/dot_general | solution.py:32
  167.6 0.0 reduce-scatter.2.cloned.1.call-update
  167.6 0.0 copy-start.7
  167.7 0.0 copy-start.8
  167.7 0.0 all-gather.8.cloned.1.call-start
  167.7 31.1 %reduce-scatter.2.cloned.1.call-done = bf16[512,1024]{1,0:T(8,128)(2,1)} async-done(((bf16[1024,1024]{1,0:T(8,128)(2,1)}), bf16[512,1024]{1,0:T(8,128)(2,1)}) %reduce-scatter.2.cloned.1.call-update) | async-done | bytes 1048592 | tf_op jit(solution)/shard_map/reduce_scatter | solution.py:35
  198.8 0.0 copy-done.2
  198.8 3.3 %fusion.1 = (bf16[512,1024]{1,0:T(8,128)(2,1)}, f32[512,1024]{1,0:T(8,128)}) fusion(f32[512,1024]{1,0:T(8,128)S(1)} %copy-done.2, bf16[512,1024]{1,0:T(8,128)(2,1)} %reduce-scatter.2.cloned.1.call-done), kind=kLoop, calls=%fused_computation.10 | loop fusion | flops 2097152 | bytes 6291456 | tf_op jit(solution)/shard_map/convert_element_type | solution.py:39
  202.2 0.0 all-gather.8.cloned.1.call-update
  202.2 33.3 %all-gather.8.cloned.1.call-done = bf16[1024,1024]{1,0:T(8,128)(2,1)} async-done(((bf16[512,1024]{1,0:T(8,128)(2,1)}), bf16[1024,1024]{1,0:T(8,128)(2,1)}) %all-gather.8.cloned.1.call-update) | async-done | bytes 2097168 | tf_op jit(solution)/shard_map/all_gather | solution.py:44
  235.5 0.0 copy-done.7
  235.5 0.0 copy-done.8
  235.5 2.3 fusion
  237.7 33.7 %psum.39 = f32[192]{0:T(256)} all-reduce(f32[192]{0:T(256)S(1)} %fusion), channel_id=1, replica_groups=mesh['dp'=2,'row'=4,'col'=4] {'row','col'}, use_global_device_ids=true, to_apply=%region_6.7 | all-reduce | flops 192 | bytes 1536 | tf_op jit(solution)/shard_map/psum | solution.py:48
  (2 shorter events, 0.0 us)
Async XLA Ops:
  7.2 1.6 copy-start.3
  7.2 1.9 copy-start.4
  7.2 3.6 %copy-start.5 = (bf16[48,1024]{1,0:T(8,128)(2,1)S(1)}, bf16[48,1024]{1,0:T(8,128)(2,1)}, u32[]{:S(2)}) copy-start(bf16[48,1024]{1,0:T(8,128)(2,1)} %param.7) | copy-start | bytes 294916
  7.2 48.3 %all-gather.4.cloned.1.call-start = ((), (), s32[]{:S(2)}) async-start(), calls=%async_computation.1 | async-start | bytes 3145728 | tf_op jit(solution)/shard_map/all_gather | solution.py:28
  7.9 19.1 %copy-start.6 = (bf16[48,1024]{1,0:T(8,128)(2,1)S(1)}, bf16[48,1024]{1,0:T(8,128)(2,1)}, u32[]{:S(2)}) copy-start(bf16[48,1024]{1,0:T(8,128)(2,1)} %param.12) | copy-start | bytes 294916
  7.9 72.2 %all-gather.6.cloned.1.call-start = ((), (), s32[]{:S(2)}) async-start(), calls=%async_computation.2 | async-start | bytes 3145728 | tf_op jit(solution)/shard_map/all_gather | solution.py:29
  8.7 109.1 %all-reduce.5.cloned.1.call-start = ((), (), s32[]{:S(2)}) async-start(), calls=%async_computation.5 | async-start | bytes 1572864 | tf_op jit(solution)/shard_map/psum | solution.py:12
  55.5 3.3 %copy-start.1 = (bf16[1024,1024]{1,0:T(8,128)(2,1)S(1)}, bf16[1024,1024]{1,0:T(8,128)(2,1)}, u32[]{:S(2)}) copy-start(bf16[1024,1024]{1,0:T(8,128)(2,1)} %all-gather.4.cloned.1.call-done) | copy-start | bytes 6291460
  60.1 104.2 %all-reduce.7.cloned.1.call-start = ((), (), s32[]{:S(2)}) async-start(), calls=%async_computation.6 | async-start | bytes 1572864 | tf_op jit(solution)/shard_map/psum | solution.py:24
  80.1 3.1 %copy-start = (bf16[1024,1024]{1,0:T(8,128)(2,1)S(1)}, bf16[1024,1024]{1,0:T(8,128)(2,1)}, u32[]{:S(2)}) copy-start(bf16[1024,1024]{1,0:T(8,128)(2,1)} %all-gather.6.cloned.1.call-done) | copy-start | bytes 6291460
  84.5 114.3 %reduce-scatter.2.cloned.1.call-start = ((), (), s32[]{:S(2)}) async-start(), calls=%async_computation.3 | async-start | bytes 3145728 | tf_op jit(solution)/shard_map/reduce_scatter | solution.py:35
  164.3 34.5 %copy-start.2 = (f32[512,1024]{1,0:T(8,128)S(1)}, f32[512,1024]{1,0:T(8,128)}, u32[]{:S(2)}) copy-start(f32[512,1024]{1,0:T(8,128)} %param.11) | copy-start | bytes 6291460
  167.6 67.8 %copy-start.7 = (bf16[192,1024]{1,0:T(8,128)(2,1)S(1)}, bf16[192,1024]{1,0:T(8,128)(2,1)}, u32[]{:S(2)}) copy-start(bf16[192,1024]{1,0:T(8,128)(2,1)} %get-tuple-element.3) | copy-start | bytes 1179652
  167.7 67.8 %copy-start.8 = (bf16[192,1024]{1,0:T(8,128)(2,1)S(1)}, bf16[192,1024]{1,0:T(8,128)(2,1)}, u32[]{:S(2)}) copy-start(bf16[192,1024]{1,0:T(8,128)(2,1)} %get-tuple-element.5) | copy-start | bytes 1179652
  167.7 67.8 %all-gather.8.cloned.1.call-start = ((), (), s32[]{:S(2)}) async-start(), calls=%async_computation.4 | async-start | bytes 3145728 | tf_op jit(solution)/shard_map/all_gather | solution.py:44
Sparse Core Ops, SparseCore 0:
  9.6 35.7 all-gather.3
  47.0 33.1 all-gather.5
  83.1 34.6 all-reduce.4
  120.1 44.1 all-reduce.6
  167.8 31.0 reduce-scatter.1
  202.3 33.1 all-gather.7
where the time goes:
time: 279 us; the launch traced here: 278 us
  waiting for transfers between devices  165 us (59%)
  blocking collectives  78.4 us (28%)
  matrix products  14.6 us (5%)
  between operations  14.2 us (5%)
  other arithmetic  3.31 us (1%)
    psum x1, waiting for transfers between devices, rotate_in(): return lax.psum(partial_sum.astype(jnp.bfloat16), 'row')  46.5 us
    psum x1, blocking collectives, per_device(): scores = lax.psum(partial_scores, ('row', 'col'))  33.7 us
    all_gather x1, waiting for transfers between devices, per_device(): lax.all_gather(shared, 'dp', axis=0, tiled=True)  33.3 us
    psum x1, waiting for transfers between devices, rotate_out(): return lax.psum(partial_sum.astype(jnp.bfloat16), 'col')  33.2 us
    all_gather x2, blocking collectives, rotate_out(): gathered = lax.all_gather(tok_rows, 'row', axis=0, tiled=True)  31.7 us
    reduce_scatter x1, waiting for transfers between devices, per_device(): lax.psum_scatter(partial_grad.astype(jnp.bfloat16), 'dp', scatter_dimensi...  31.1 us
    all_gather x1, waiting for transfers between devices, per_device(): panel_in = lax.all_gather(in_basis, 'dp', axis=0, tiled=True)  20 us
    all_gather x2, blocking collectives, rotate_in(): gathered = lax.all_gather(picked, 'col', axis=0, tiled=True)  13 us
  transfers between devices with their start and end apart: 6, of which 5 were waited for; matrix products, arithmetic and copies ran while one was open for 4% of the time, Pallas kernels for 0%

commit v1 on v0

--- a/solution.py
+++ b/solution.py
@@ -24,7 +24,7 @@
     return lax.psum(partial_sum.astype(jnp.bfloat16), "row")
 
 
-def per_device(query_out, query_in, out_basis, in_basis, eigvals, train_out, train_in):
+def wide_plan(query_out, query_in, out_basis, in_basis, eigvals, train_out, train_in):
     panel_out = lax.all_gather(out_basis, "dp", axis=1, tiled=True)
     panel_in = lax.all_gather(in_basis, "dp", axis=0, tiled=True)
     query_rot = rotate_out(query_out, panel_out)
@@ -49,6 +49,33 @@
     return (precond, scores)
 
 
+def local_plan(query_out, query_in, out_basis, in_basis, eigvals, train_out, train_in):
+    groups = lax.axis_size("dp")
+    row_count = lax.axis_size("row")
+    own = query_out.shape[0]
+    stacked = jnp.stack([query_out, train_out])
+    out_rows = lax.all_gather(stacked, ("dp", "row"), axis=1, tiled=True)
+    sub_width = query_in.shape[1] // (groups * row_count)
+    in_stack = jnp.stack([query_in, train_in]).reshape(2, own, groups, row_count, sub_width)
+    picked = lax.dynamic_index_in_dim(in_stack, lax.axis_index("row"), 3, keepdims=False)
+    in_rows = lax.all_gather(picked, ("dp", "col"), axis=1, tiled=True)
+    in_rows = lax.dynamic_index_in_dim(in_rows, lax.axis_index("dp"), 2, keepdims=False)
+    tokens = out_rows.shape[1]
+    out_part = jnp.dot(out_rows.reshape(2 * tokens, -1), out_basis, preferred_element_type=jnp.float32)
+    in_part = jnp.dot(in_rows.reshape(2 * tokens, -1), in_basis, preferred_element_type=jnp.float32)
+    rot = lax.psum(out_part.astype(jnp.bfloat16), "col")
+    inr = lax.psum(in_part.astype(jnp.bfloat16), ("dp", "row"))
+    grad = lax.dot_general(
+        rot[:tokens], inr[:tokens], (((0,), (0,)), ((), ())), preferred_element_type=jnp.float32
+    )
+    precond = grad / (eigvals + damping)
+    mixed = jnp.dot(rot[tokens:], precond.astype(jnp.bfloat16), preferred_element_type=jnp.float32)
+    partial_scores = jnp.sum(mixed * inr[tokens:].astype(jnp.float32), axis=1)
+    total = lax.psum(partial_scores, ("dp", "row", "col"))
+    kept = tokens // groups
+    return (precond, lax.dynamic_slice_in_dim(total, lax.axis_index("dp") * kept, kept))
+
+
 def solution(mesh):
     in_specs = (
         P(("dp", "row"), "col"),
@@ -61,5 +88,5 @@
     )
     out_specs = (P(("dp", "row"), "col"), P("dp"))
     return jax.shard_map(
-        per_device, mesh=mesh, in_specs=in_specs, out_specs=out_specs, check_vma=False
+        local_plan if mesh.shape["dp"] <= 2 else wide_plan, mesh=mesh, in_specs=in_specs, out_specs=out_specs, check_vma=False
     )

time: 279 us -> 272 us (0.975)
  blocking collectives: 78.4 us -> 39.9 us
  waiting for transfers between devices: 165 us -> 200 us
  matrix products: 14.6 us -> 8.94 us
  local copies, waits for them, and re-layouts: 1.99 us -> 6.18 us
    psum x2, waiting for transfers between devices: 79.7 us -> 125 us  [the longest x1 93 us: local_plan(): inr = lax.psum(in_part.astype(jnp.bfloat16), ('dp', 'row'))]
    all_gather x4 -> x0, blocking collectives: 44.7 us -> none  [the longest x2 31.7 us: rotate_out(): gathered = lax.all_gather(tok_rows, 'row', axis=0, tiled=True)]
    reduce_scatter x1 -> x0, waiting for transfers between devices: 31.1 us -> none  [per_device(): lax.psum_scatter(partial_grad.astype(jnp.bfloat16), 'dp', scatter_dimensi...]
    all_gather x3 -> x2, waiting for transfers between devices: 53.2 us -> 75.3 us  [the longest x1 45 us: local_plan(): out_rows = lax.all_gather(stacked, ('dp', 'row'), axis=1, tiled=True)]
    psum x1, blocking collectives: 33.7 us -> 39.9 us  [local_plan(): total = lax.psum(partial_scores, ('dp', 'row', 'col'))]
    dot_general x6 -> x4, matrix products: 14.6 us -> 8.94 us  [the longest x1 3.3 us: local_plan(): jnp.dot(out_rows.reshape(2 * tokens, -1), out_basis, preferred_element_ty...]
    convert_element_type x1 -> x0, other arithmetic: 3.31 us -> none  [per_device(): shared = precond.astype(jnp.bfloat16)]
    another operation x0 -> x2, other arithmetic: none -> 3.02 us  [the longest x1 1.76 us: local_plan(): stacked = jnp.stack([query_out, train_out])]
  transfers between devices with their start and end apart: 6 -> 4, of which waited for: 5 -> 4; matrix products, arithmetic and copies ran while one was open for 4% -> 4% of each run, Pallas kernels for 0% -> 0%
where the time goes in v1:
time: 272 us
  waiting for transfers between devices  200 us (74%)
  blocking collectives  39.9 us (15%)
  between operations  13.9 us (5%)
  matrix products  8.94 us (3%)
  local copies, waits for them, and re-layouts  6.18 us (2%)
  other arithmetic  3.02 us (1%)
    psum x1, waiting for transfers between devices, local_plan(): inr = lax.psum(in_part.astype(jnp.bfloat16), ('dp', 'row'))  93 us
    all_gather x1, waiting for transfers between devices, local_plan(): out_rows = lax.all_gather(stacked, ('dp', 'row'), axis=1, tiled=True)  45 us
    psum x1, blocking collectives, local_plan(): total = lax.psum(partial_scores, ('dp', 'row', 'col'))  39.9 us
    psum x1, waiting for transfers between devices, local_plan(): rot = lax.psum(out_part.astype(jnp.bfloat16), 'col')  31.6 us
    all_gather x1, waiting for transfers between devices, local_plan(): in_rows = lax.all_gather(picked, ('dp', 'col'), axis=1, tiled=True)  30.3 us
  transfers between devices with their start and end apart: 4, of which 4 were waited for; matrix products, arithmetic and copies ran while one was open for 4% of the time, Pallas kernels for 0%

profile of v1, /device:TPU:0, one launch (start us, length us, event | category | flops | bytes accessed | tf_op | source)
XLA Modules:
  0.0 272.0 jit_solution(13352617255220400935)
XLA Ops:
  7.2 0.0 copy-start
  7.2 0.0 copy-start.2
  7.2 0.0 all-gather.4.cloned.1.call-start
  7.2 1.8 pad_maximum_fusion
  9.0 0.0 all-gather.4.cloned.1.call-update
  9.0 0.0 all-gather.6.cloned.1.call-start
  9.1 0.0 copy-start.5
  9.1 1.4 stack.21
  10.5 0.0 copy-done.2
  10.5 0.3 stack.22
  10.8 1.3 fusion.2
  12.0 0.0 all-gather.6.cloned.1.call-update
  12.0 0.0 all-reduce.3.cloned.1.call-start
  12.1 45.0 %all-gather.4.cloned.1.call-done = bf16[2,384,1024]{2,1,0:T(8,128)(2,1)} async-done(((bf16[2,48,1024]{2,1,0:T(8,128)(2,1)}), bf16[2,384,1024]{2,1,0:T(8,128)(2,1)}) %all-gather.4.cloned.1.call-update) | async-done | bytes 1572880 | tf_op jit(solution)/shard_map/all_gather | solution.py:57
  57.1 0.0 copy-done.5
  57.1 3.3 %convolution_convert_fusion.1 = bf16[768,512]{1,0:T(8,128)(2,1)} fusion(bf16[768,1024]{1,0:T(8,128)(2,1)} %bitcast.11, bf16[1024,512]{1,0:T(8,128)(2,1)S(1)} %copy-done.5), kind=kOutput, calls=%fused_computation.3 | convolution fusion | flops 805699584 | bytes 3407872 | tf_op jit(solution)/shard_map/dot_general | solution.py:64
  60.4 0.0 all-reduce.3.cloned.1.call-update
  60.4 0.0 all-reduce.5.cloned.1.call-start
  60.5 30.3 %all-gather.6.cloned.1.call-done = bf16[2,384,2,1,512]{4,3,2,1,0:T(2,128)(2,1)} async-done(((bf16[2,48,2,1,512]{4,3,2,1,0:T(2,128)(2,1)}), bf16[2,384,2,1,512]{4,3,2,1,0:T(2,128)(2,1)}) %all-gather.6.cloned.1.call-update) | async-done | bytes 1572880 | tf_op jit(solution)/shard_map/all_gather | solution.py:61
  90.7 3.0 %constant_dynamic-slice_fusion = bf16[2,384,1,1,512]{4,3,2,1,0:T(2,128)(2,1)S(1)} fusion(bf16[2,384,2,1,512]{4,3,2,1,0:T(2,128)(2,1)} %all-gather.6.cloned.1.call-done, s32[]{:T(128)S(6)} %select_n.12), kind=kLoop, calls=%fused_computation.12 | loop fusion | bytes 1572868 | tf_op jit(solution)/shard_map/jit(dynamic_index_in_dim)/dynamic_slice | solution.py:62
  93.8 0.2 copy.9
  94.0 0.0 copy-done
  94.0 2.1 convolution_convert_fusion
  96.1 0.0 all-reduce.5.cloned.1.call-update
  96.2 31.6 %all-reduce.3.cloned.1.call-done = bf16[768,512]{1,0:T(8,128)(2,1)} async-done(((bf16[768,512]{1,0:T(8,128)(2,1)}), bf16[768,512]{1,0:T(8,128)(2,1)}) %all-reduce.3.cloned.1.call-update) | async-done | bytes 786448 | tf_op jit(solution)/shard_map/psum | solution.py:66
  127.8 93.0 %all-reduce.5.cloned.1.call-done = bf16[768,1024]{1,0:T(8,128)(2,1)} async-done(((bf16[768,1024]{1,0:T(8,128)(2,1)}), bf16[768,1024]{1,0:T(8,128)(2,1)}) %all-reduce.5.cloned.1.call-update) | async-done | bytes 1572880 | tf_op jit(solution)/shard_map/psum | solution.py:67
  220.8 0.0 copy-start.3
  220.8 0.0 copy-start.4
  220.8 2.8 %add_divide_fusion = f32[512,1024]{1,0:T(8,128)S(1)} fusion(f32[512,1024]{1,0:T(8,128)} %param.11, bf16[768,1024]{1,0:T(8,128)(2,1)} %all-reduce.5.cloned.1.call-done, bf16[768,512]{1,0:T(8,128)(2,1)} %all-reduce.3.cloned.1.call-done), kind=kOutput, calls=%fused_computation | convolution fusion | flops 403701760 | bytes 5373952 | tf_op jit(solution)/shard_map/dot_general | solution.py:68
  223.6 0.0 copy-done.3
  223.6 0.0 copy-done.4
  223.6 0.0 copy-start.1
  223.6 0.7 multiply_reduce_fusion
  224.3 0.6 copy-done.1
  224.9 39.9 %psum.23 = f32[384]{0:T(512)S(1)} all-reduce(f32[384]{0:T(512)S(1)} %multiply_reduce_fusion), channel_id=1, replica_groups=mesh['dp'=2,'row'=4,'col'=4] {'dp','row','col'}, use_global_device_ids=true, to_apply=%region_3.4 | all-reduce | flops 384 | bytes 3072 | tf_op jit(solution)/shard_map/psum | solution.py:74
  264.9 0.6 dynamic_slice.13
Async XLA Ops:
  7.2 86.8 %copy-start = (bf16[512,1024]{1,0:T(8,128)(2,1)S(1)}, bf16[512,1024]{1,0:T(8,128)(2,1)}, u32[]{:S(2)}) copy-start(bf16[512,1024]{1,0:T(8,128)(2,1)} %param.10) | copy-start | bytes 3145732
  7.2 3.3 %copy-start.2 = (bf16[48,4096]{1,0:T(8,128)(2,1)S(1)}, bf16[48,4096]{1,0:T(8,128)(2,1)}, u32[]{:S(2)}) copy-start(bf16[48,4096]{1,0:T(8,128)(2,1)} %param.13) | copy-start | bytes 1179652
  7.2 49.9 %all-gather.4.cloned.1.call-start = ((), (), s32[]{:S(2)}) async-start(), calls=%async_computation | async-start | bytes 1769472 | tf_op jit(solution)/shard_map/all_gather | solution.py:57
  9.0 81.7 %all-gather.6.cloned.1.call-start = ((), (), s32[]{:S(2)}) async-start(), calls=%async_computation.3 | async-start | bytes 3538944 | tf_op jit(solution)/shard_map/all_gather | solution.py:61
  9.1 48.0 %copy-start.5 = (bf16[1024,512]{1,0:T(8,128)(2,1)S(1)}, bf16[1024,512]{1,0:T(8,128)(2,1)}, u32[]{:S(2)}) copy-start(bf16[1024,512]{1,0:T(8,128)(2,1)} %param.9) | copy-start | bytes 3145732
  12.0 115.7 %all-reduce.3.cloned.1.call-start = ((), (), s32[]{:S(2)}) async-start(), calls=%async_computation.1 | async-start | bytes 1572864 | tf_op jit(solution)/shard_map/psum | solution.py:66
  60.4 160.3 %all-reduce.5.cloned.1.call-start = ((), (), s32[]{:S(2)}) async-start(), calls=%async_computation.2 | async-start | bytes 3145728 | tf_op jit(solution)/shard_map/psum | solution.py:67
  220.8 2.8 %copy-start.3 = (bf16[768,1024]{1,0:T(8,128)(2,1)S(1)}, bf16[768,1024]{1,0:T(8,128)(2,1)}, u32[]{:S(2)}) copy-start(bf16[768,1024]{1,0:T(8,128)(2,1)} %all-reduce.5.cloned.1.call-done) | copy-start | bytes 4718596
  220.8 2.8 %copy-start.4 = (bf16[768,512]{1,0:T(8,128)(2,1)S(1)}, bf16[768,512]{1,0:T(8,128)(2,1)}, u32[]{:S(2)}) copy-start(bf16[768,512]{1,0:T(8,128)(2,1)} %all-reduce.3.cloned.1.call-done) | copy-start | bytes 2359300
  223.6 1.3 copy-start.1
Sparse Core Ops, SparseCore 0:
  10.2 46.8 all-gather.3
  59.6 31.1 all-gather.5
  93.1 34.6 all-reduce.2
  131.7 89.0 all-reduce.4
